TPU v7x, 32 devices: a whole 2x2x4 slice. The times are simulated.
32 devices in a mesh: group: 2 (over x), tile: 16 (over z, y, core).
Axes of the slice: x: 2, y: 2, z: 4, core: 2. Of those that a mesh axis runs over, the one named last changes fastest.
Arguments:
- samples: bfloat16 [2, 1024, 65984], P(None, ('group', 'tile')), parts along dimension 1, may hold values from -6 to 6
- fir_taps: float32 [8, 64], replicated, may hold values from -2 to 2
- chan_map: int32 [32], replicated, may hold values from 0 to 63, as said below
- layout: int32 [10], replicated, may hold values from 0 to 9, each once
Outputs:
- visibilities: float32 [640, 2, 128, 128], P(('group', 'tile')), parts along dimension 0
There are 2 independent parts, one for each index of `group`. A program takes and returns all parts, laid end to end along the dimension named above; an argument that names none is the same for every part. Nothing has to cross between parts.
Inputs may be any that keep to these rules, and one draw needn't show every extreme that they name: `chan_map`: 32 distinct channels in increasing order; channels 0 and 63 are always kept. `layout`: each block pair once.
All inputs are finite; a program needn't handle non-finite values.
Results may differ from a plain program's by a relative error of at most 0.0033.
Values may be sent and summed in bfloat16 or wider, within the bound.
A program may use at most 128 MiB of HBM per device.

v0:
```python
import math

import jax
import jax.numpy as jnp
import numpy as np
from jax import lax
from jax.sharding import PartitionSpec as P

NCHAN = 64
KEEP = 32
TAPS = 8
BLOCK = 128
CH = 4
NBLK = 4
NPAIR = 10


def swapped_2(block, axis, stride):
    count = lax.axis_size(axis)
    route = []
    for low in range(count):
        high = low | 1 << stride
        if high != low and high < count:
            route += [(low, high), (high, low)]
    return lax.ppermute(block, axis, route)


def pair_tables(block_count):
    first_block = []
    second_block = []
    for i in range(block_count):
        for j in range(i, block_count):
            first_block.append(i)
            second_block.append(j)
    return (np.array(first_block, np.int32), np.array(second_block, np.int32))


def dft_table(channels):
    tap_index = jnp.arange(NCHAN, dtype=jnp.int32).reshape((NCHAN,) + (1,) * channels.ndim)
    phases = tap_index * channels[None] % NCHAN
    angles = phases.astype(jnp.float32) * (2.0 * math.pi / NCHAN)
    scaling = 1.0 / math.sqrt(NCHAN)
    cosine = jnp.cos(angles) * scaling
    sine_part = jnp.sin(angles) * scaling
    real_rows = jnp.stack([cosine, -sine_part], 1)
    imag_rows = jnp.stack([sine_part, cosine], 1)
    return jnp.stack([real_rows, imag_rows], 0).astype(jnp.bfloat16)


def weigh(samples, fir_taps, spec_count):
    summed = jnp.zeros(samples.shape[:2] + (spec_count * NCHAN,), jnp.float32)
    for k in range(TAPS):
        window = lax.slice_in_dim(
            samples, k * NCHAN, k * NCHAN + spec_count * NCHAN, axis=2
        ).astype(jnp.float32)
        summed = summed + window * jnp.tile(fir_taps[k], spec_count)
    return summed.astype(jnp.bfloat16)


def lookup(positions, table_values):
    onehot = positions[:, None] == jnp.arange(table_values.shape[0], dtype=jnp.int32)[None, :]
    return jnp.sum(jnp.where(onehot, table_values[None, :], 0), 1).astype(jnp.int32)


def on_device(samples, fir_taps, chan_map, layout):
    tile_count = lax.axis_size("tile")
    in_dev = samples.shape[1]
    input_total = in_dev * tile_count
    spec_count = samples.shape[2] // NCHAN - TAPS + 1
    weighted = weigh(samples, fir_taps, spec_count)
    first_block, second_block = pair_tables(NBLK)
    first_table = jnp.asarray(first_block)
    second_table = jnp.asarray(second_block)
    tb_count = tile_count * CH // KEEP
    time_len = spec_count // tb_count
    first_sel = lookup(layout, first_table)
    second_sel = lookup(layout, second_table)
    dft_rows = dft_table(chan_map.reshape(KEEP // CH, CH))
    frames = weighted.reshape(2, in_dev, tb_count, time_len, NCHAN)
    spectra = jnp.einsum(
        "rnqoc,ribtn->obiqct", dft_rows, frames, preferred_element_type=jnp.float32
    )
    spectra = spectra.astype(jnp.bfloat16).reshape(tile_count, in_dev, 2, CH, time_len)
    received = lax.all_to_all(spectra, "tile", split_axis=0, concat_axis=1, tiled=True)
    c_items = received.shape[3]
    flat_inputs = received.reshape(input_total, 2, c_items, time_len)
    swapped = jnp.stack([-flat_inputs[:, 1], flat_inputs[:, 0]], 1)
    real_full = jnp.einsum(
        "apct,bpct->cab", flat_inputs, flat_inputs, preferred_element_type=jnp.float32
    )
    imag_full = jnp.einsum(
        "apct,bpct->cab", flat_inputs, swapped, preferred_element_type=jnp.float32
    )
    real_full = real_full.reshape(c_items, NBLK, BLOCK, NBLK, BLOCK)
    imag_full = imag_full.reshape(c_items, NBLK, BLOCK, NBLK, BLOCK)
    real_blocks = real_full[:, first_sel, :, second_sel, :]
    imag_blocks = imag_full[:, first_sel, :, second_sel, :]
    stacked = jnp.stack([real_blocks, imag_blocks], 2)
    partial_terms = jnp.swapaxes(stacked, 0, 1)
    row_terms = partial_terms.reshape(CH * NPAIR, 2, BLOCK, BLOCK)
    time_slot = lax.axis_index("tile") % tb_count
    level_count = tb_count.bit_length() - 1
    for bit_level in range(level_count - 1, -1, -1):
        half_rows = row_terms.shape[0] // 2
        upper_bit = time_slot // (1 << bit_level) % 2
        kept_rows = lax.dynamic_slice_in_dim(row_terms, upper_bit * half_rows, half_rows, 0)
        sent_rows = lax.dynamic_slice_in_dim(row_terms, (1 - upper_bit) * half_rows, half_rows, 0)
        row_terms = kept_rows + swapped_2(sent_rows, "tile", bit_level)
    return row_terms / spec_count


def solution(mesh):
    placed = (P(None, ("group", "tile"), None), P(), P(), P())
    return jax.shard_map(
        on_device,
        mesh=mesh,
        in_specs=placed,
        out_specs=P(("group", "tile"), None, None, None),
        check_vma=False,
    )
```

profile of v0, /device:TPU:15, one launch (start us, length us, event | category | flops | bytes accessed | tf_op | source)
XLA Modules:
  0.0 224.4 jit_solution(8689402433933781313)
XLA Ops:
  0.0 1.0 slice_bitcast_fusion.7
  1.0 0.1 mul.161
  1.2 0.1 mul.164
  1.4 0.1 mul.167
  1.6 0.1 mul.170
  1.8 0.1 mul.173
  1.9 0.1 mul.176
  2.1 0.1 mul.179
  2.3 0.1 mul.182
  2.5 34.4 %add_convert_fusion = bf16[2,32,65536]{2,1,0:T(8,128)(2,1)} fusion(f32[65536]{0:T(1024)S(1)} %mul.182, bf16[2,32,65984]{2,1,0:T(8,128)(2,1)} %param.6, f32[65536]{0:T(1024)S(1)} %mul.179, f32[65536]{0:T(1024)S(1)} %mul.176, f32[65536]{0:T(1024)S(1)} %mul.173, f32[65536]{0:T(1024)S(1)} %mul.170, f32[65536]{0:T(1024)S(1)} %mul.167, f32[65536]{0:T(1024)S(1)} %mul.164, ...), kind=kLoop, calls=%fused_computation.4 | loop fusion | flops 100663296 | bytes 77594624 | tf_op jit(solution)/shard_map/convert_element_type | solution.py:57
  36.9 0.0 copy-start.1
  36.9 18.2 %reshape.121 = bf16[2,32,2,512,64]{4,3,2,1,0:T(8,128)(2,1)} reshape(bf16[2,32,65536]{2,1,0:T(8,128)(2,1)} %add_convert_fusion) | data formatting | bytes 16777216 | tf_op jit(solution)/shard_map/reshape | solution.py:79
  55.1 0.0 copy-done.1
  55.1 0.1 mul.186
  55.1 0.1 copy.26
  55.2 0.2 negate_convert_fusion
  55.4 10.9 %fusion.2 = bf16[8,2,32,2,4,512]{5,0,4,3,1,2:T(8,128)(2,1)S(1)} fusion(bf16[1,64,2,8,4]{1,3,0,4,2:T(8,128)(2,1)S(1)} %get-tuple-element.10, bf16[1,64,2,8,4]{1,3,0,4,2:T(8,128)(2,1)S(1)} %get-tuple-element.9, bf16[2,32,2,512,64]{4,3,2,1,0:T(8,128)(2,1)} %reshape.121), kind=kOutput, calls=%fused_computation.7 | convolution fusion | flops 539000832 | bytes 12599296 | tf_op jit(solution)/shard_map/rnqoc,ribtn->obiqct/dot_general | solution.py:80
  66.3 4.4 %copy.29 = bf16[8,2,32,2,4,512]{5,2,4,3,1,0:T(8,128)(2,1)} copy(bf16[8,2,32,2,4,512]{5,0,4,3,1,2:T(8,128)(2,1)S(1)} %fusion.2) | data formatting | bytes 8388608 | tf_op jit(solution)/shard_map/convert_element_type | solution.py:83
  70.6 0.0 copy-start.2
  70.6 0.0 copy-start.3
  70.6 0.0 copy-start.4
  70.7 6.7 %all-to-all-start = ((bf16[16,32,2,4,512]{4,1,3,2,0:T(8,128)(2,1)}), bf16[16,32,2,4,512]{4,1,3,2,0:T(8,128)(2,1)}, u32[]{:S(2)}, u32[]{:S(2)}) async-start(bf16[16,32,2,4,512]{4,1,3,2,0:T(8,128)(2,1)} %bitcast.66), calls=%async_computation | async-start | bytes 8388608 | tf_op jit(solution)/shard_map/all_to_all | solution.py:84
  77.3 0.0 copy-done.2
  77.3 0.0 copy-done.3
  77.4 0.0 copy-done.4
  77.4 0.2 select_reduce_fusion.1
  77.6 92.2 %all-to-all-done = bf16[16,32,2,4,512]{4,1,3,2,0:T(8,128)(2,1)} async-done(((bf16[16,32,2,4,512]{4,1,3,2,0:T(8,128)(2,1)}), bf16[16,32,2,4,512]{4,1,3,2,0:T(8,128)(2,1)}, u32[]{:S(2)}, u32[]{:S(2)}) %all-to-all-start) | async-done | bytes 4194336 | tf_op jit(solution)/shard_map/all_to_all | solution.py:84
  169.8 2.5 %copy.30 = bf16[16,32,2,4,512]{4,1,0,2,3:T(8,128)(2,1)S(1)} copy(bf16[16,32,2,4,512]{4,1,3,2,0:T(8,128)(2,1)} %all-to-all-done) | data formatting | bytes 8388608 | tf_op jit(solution)/shard_map/all_to_all | solution.py:84
  172.3 0.3 slice_negate_fusion
  172.6 4.3 %convolution_bitcast_fusion = f32[4,512,512]{2,1,0:T(8,128)} fusion(bf16[512,2,4,512]{3,0,1,2:T(8,128)(2,1)S(1)} %bitcast.68), kind=kOutput, calls=%fused_computation.14 | convolution fusion | flops 2147483648 | bytes 8388608 | tf_op jit(solution)/shard_map/apct,bpct->cab/dot_general | solution.py:88
  176.9 4.4 %fusion.9 = f32[4,512,512]{2,1,0:T(8,128)} fusion(bf16[512,2,4,512]{3,0,1,2:T(8,128)(2,1)S(1)} %bitcast.69, bf16[512,1,4,512]{3,0,1,2:T(8,128)(2,1)S(1)} %get-tuple-element.8, bf16[512,1,4,512]{3,0,1,2:T(8,128)(2,1)S(1)} %get-tuple-element.7), kind=kOutput, calls=%fused_computation.13 | convolution fusion | flops 2149580800 | bytes 12582912 | tf_op jit(solution)/shard_map/apct,bpct->cab/dot_general | solution.py:91
  181.2 5.3 %reshape.125 = f32[4,4,128,4,128]{4,3,2,1,0:T(4,128)} reshape(f32[4,512,512]{2,1,0:T(8,128)} %fusion.9) | data formatting | bytes 8388608 | tf_op jit(solution)/shard_map/reshape | solution.py:95
  186.5 4.8 %copy.32 = f32[4,4,128,4,128]{4,2,3,1,0:T(8,128)} copy(f32[4,4,128,4,128]{4,3,2,1,0:T(4,128)} %reshape.125) | data formatting | bytes 8388608 | tf_op jit(solution)/shard_map/reshape | solution.py:95
  191.3 5.3 %reshape.124 = f32[4,4,128,4,128]{4,3,2,1,0:T(4,128)} reshape(f32[4,512,512]{2,1,0:T(8,128)} %convolution_bitcast_fusion) | data formatting | bytes 8388608 | tf_op jit(solution)/shard_map/reshape | solution.py:94
  196.6 4.7 %copy.31 = f32[4,4,128,4,128]{4,2,3,1,0:T(8,128)} copy(f32[4,4,128,4,128]{4,3,2,1,0:T(4,128)} %reshape.124) | data formatting | bytes 8388608 | tf_op jit(solution)/shard_map/reshape | solution.py:94
  201.3 2.9 %gather_fusion.1 = f32[10,4,128,128]{3,2,1,0:T(8,128)S(1)} fusion(f32[4,4,128,4,128]{4,2,3,1,0:T(8,128)} %copy.32, s32[10]{0:T(128)S(1)} %fusion.26), kind=kCustom, calls=%fused_computation.1 | custom fusion | bytes 5242960 | tf_op jit(solution)/shard_map/gather | solution.py:97
  204.2 4.5 %gather_fusion = f32[10,4,128,128]{3,2,1,0:T(8,128)} fusion(f32[4,4,128,4,128]{4,2,3,1,0:T(8,128)} %copy.31, s32[10]{0:T(128)S(1)} %fusion.26), kind=kCustom, calls=%fused_computation | custom fusion | bytes 5242960 | tf_op jit(solution)/shard_map/gather | solution.py:96
  208.7 2.2 maximum_bitcast_fusion
  210.9 0.6 copy.33
  211.5 0.0 copy-start
  211.6 2.3 %copy-done = f32[4,10,2,128,128]{4,3,2,1,0:T(8,128)} copy-done((f32[4,10,2,128,128]{4,3,2,1,0:T(8,128)}, f32[4,10,2,128,128]{4,3,2,1,0:T(8,128)S(1)}, u32[]{:S(2)}) %copy-start) | copy-done | bytes 5242904
  213.9 1.8 constant_dynamic-slice_fusion
  215.6 0.2 collective-permute-start
  215.9 4.9 %collective-permute-done = f32[20,2,128,128]{3,2,1,0:T(8,128)S(1)} collective-permute-done((f32[20,2,128,128]{3,2,1,0:T(8,128)}, f32[20,2,128,128]{3,2,1,0:T(8,128)S(1)}, u32[]{:S(2)}, u32[]{:S(2)}) %collective-permute-start) | collective-permute-done | bytes 2621472 | tf_op jit(solution)/shard_map/ppermute | solution.py:25
  220.8 3.7 %add_multiply_fusion = f32[20,2,128,128]{3,2,1,0:T(8,128)} fusion(f32[20,2,128,128]{3,2,1,0:T(8,128)S(1)} %collective-permute-done, f32[40,2,128,128]{3,2,1,0:T(8,128)} %bitcast.65, s32[]{:T(128)S(6)} %select_n.76), kind=kLoop, calls=%fused_computation.12 | loop fusion | flops 1310720 | bytes 7864324 | tf_op jit(solution)/shard_map/div | solution.py:109
  (10 shorter events, 0.3 us)
Async XLA Ops:
  36.9 18.2 %copy-start.1 = (s32[32]{0:T(128)S(1)}, s32[32]{0:T(128)}, u32[]{:S(2)}) copy-start(s32[32]{0:T(128)} %param.8) | copy-start | bytes 388
  70.6 6.7 %copy-start.2 = (s32[10]{0:T(128)S(1)}, s32[10]{0:T(128)}, u32[]{:S(2)}) copy-start(s32[10]{0:T(128)} %param.9) | copy-start | bytes 124
  70.6 6.7 %copy-start.3 = (s32[10]{0:T(128)S(1)}, s32[10]{0:T(128)}, u32[]{:S(2)}) copy-start(s32[10]{0:T(128)} %constant.65.clone) | copy-start | bytes 124
  70.6 6.7 %copy-start.4 = (s32[10]{0:T(128)S(1)}, s32[10]{0:T(128)}, u32[]{:S(2)}) copy-start(s32[10]{0:T(128)} %constant.66.clone) | copy-start | bytes 124
  70.7 99.2 %all-to-all-start = ((bf16[16,32,2,4,512]{4,1,3,2,0:T(8,128)(2,1)}), bf16[16,32,2,4,512]{4,1,3,2,0:T(8,128)(2,1)}, u32[]{:S(2)}, u32[]{:S(2)}) async-start(bf16[16,32,2,4,512]{4,1,3,2,0:T(8,128)(2,1)} %bitcast.66), calls=%async_computation | async-start | bytes 8388608 | tf_op jit(solution)/shard_map/all_to_all | solution.py:84
  211.5 2.3 %copy-start = (f32[4,10,2,128,128]{4,3,2,1,0:T(8,128)}, f32[4,10,2,128,128]{4,3,2,1,0:T(8,128)S(1)}, u32[]{:S(2)}) copy-start(f32[4,10,2,128,128]{4,3,2,1,0:T(8,128)S(1)} %copy.33) | copy-start | bytes 15728644
  215.6 5.1 %collective-permute-start = (f32[20,2,128,128]{3,2,1,0:T(8,128)}, f32[20,2,128,128]{3,2,1,0:T(8,128)S(1)}, u32[]{:S(2)}, u32[]{:S(2)}) collective-permute-start(f32[20,2,128,128]{3,2,1,0:T(8,128)} %constant_dynamic-slice_fusion), channel_id=1, source_target_pairs={{0,1},{1,0},{2,3},{3,2},{4,5},{5,4},{6,7},{7,6},{8,9},{9,8},{10,11... | collective-permute-start | bytes 7864328 | tf_op jit(solution)/shard_map/ppermute | solution.py:25
where the time goes:
time: 226 us; the launch traced here: 224 us
  waiting for transfers between devices  97.1 us (43%)
  local copies, waits for them, and re-layouts  59.7 us (26%)
  other arithmetic  40.9 us (18%)
  matrix products  19.5 us (9%)
  starting transfers between devices  6.91 us (3%)
    all_to_all x1, waiting for transfers between devices, on_device(): lax.all_to_all(spectra, 'tile', split_axis=0, concat_axis=1, tiled=True)  92.2 us
    convert_element_type x1, other arithmetic, weigh(): return summed.astype(jnp.bfloat16)  34.4 us
    reshape x1, local copies, waits for them, and re-layouts, on_device(): frames = weighted.reshape(2, in_dev, tb_count, time_len, NCHAN)  18.2 us
    dot_general x1, matrix products, on_device(): jnp.einsum('rnqoc,ribtn->obiqct', dft_rows, frames, preferred_element_typ...  10.9 us
    reshape x2, local copies, waits for them, and re-layouts, on_device(): imag_full = imag_full.reshape(c_items, NBLK, BLOCK, NBLK, BLOCK)  10.1 us
    reshape x2, local copies, waits for them, and re-layouts, on_device(): real_full = real_full.reshape(c_items, NBLK, BLOCK, NBLK, BLOCK)  10 us
    all_to_all x1, starting transfers between devices, on_device(): lax.all_to_all(spectra, 'tile', split_axis=0, concat_axis=1, tiled=True)  6.69 us
    ppermute x1, waiting for transfers between devices, swapped_2(): return lax.ppermute(block, axis, route)  4.89 us
  transfers between devices with their start and end apart: 2, of which 2 were waited for; matrix products, arithmetic and copies ran while one was open for 0% of the time, Pallas kernels for 0%

commit v1 on v0

v1 whole, which is shorter than its diff:
```python
import functools
import math

import jax
import jax.numpy as jnp
import numpy as np
from jax import lax
from jax.experimental import pallas as pl
from jax.experimental.pallas import tpu as pltpu
from jax.sharding import PartitionSpec as P

NCHAN = 64
KEEP = 32
TAPS = 8
BLOCK = 128
NBLK = 4
NPAIR = 10

DT = 8
STRIDE = DT * NCHAN
TAIL = (TAPS - 1) * NCHAN
WIDE = 2 * STRIDE
LANES = 128
MESH = pl.DeviceIdType.MESH
NT = (((1,), (1,)), ((), ()))


def pair_tables(block_count):
    pairs = [(i, j) for i in range(block_count) for j in range(i, block_count)]
    return tuple(np.array(side, np.int32) for side in zip(*pairs))


def dft_table(channels):
    tap_index = jnp.arange(NCHAN, dtype=jnp.int32)
    angles = (tap_index[:, None] * channels[None] % NCHAN).astype(jnp.float32) * (
        2.0 * math.pi / NCHAN
    )
    scaling = 1.0 / math.sqrt(NCHAN)
    cosine = jnp.cos(angles) * scaling
    sine_part = jnp.sin(angles) * scaling
    real_rows = jnp.stack([cosine, -sine_part], 1)
    imag_rows = jnp.stack([sine_part, cosine], 1)
    return jnp.stack([real_rows, imag_rows], 0).astype(jnp.bfloat16)


def partner(me, k, bits):
    return sum(
        ((me // (1 << b) + (k >> b & 1)) % 2) * (1 << b) for b in range(bits)
    )


def kernel(
    tiles,
    chunks,
    layout_ref,
    dft_ref,
    fir_ref,
    samples_ref,
    out_ref,
    held,
    filt,
    window,
    send,
    recv,
    left,
    right,
    total,
    load_sem,
    own_sem,
    send_sem,
    recv_sem,
):
    bits = tiles.bit_length() - 1
    me = lax.axis_index("tile")
    per = 16 * STRIDE
    inputs = samples_ref.shape[1]
    order = sorted(range(1, tiles), reverse=True)
    chans = KEEP // tiles

    def load(c):
        at = pl.ds(pl.multiple_of(c * per, per), per)
        return pltpu.make_async_copy(
            samples_ref.at[:, :, at], held.at[:, :, at], load_sem.at[c]
        )

    rest = pltpu.make_async_copy(
        samples_ref.at[:, :, pl.ds(chunks * per, TAIL)],
        held.at[:, :, pl.ds(chunks * per, TAIL)],
        load_sem.at[chunks],
    )
    for c in range(chunks):
        load(c).start()
    rest.start()

    barrier = pltpu.get_barrier_semaphore()
    for k in order:
        pl.semaphore_signal(
            barrier, inc=1, device_id={"tile": partner(me, k, bits)}, device_id_type=MESH
        )

    def out_copy(c, k):
        there = partner(me, k, bits)
        return pltpu.make_async_remote_copy(
            src_ref=send.at[c, there],
            dst_ref=recv.at[c, me],
            send_sem=send_sem.at[c, k],
            recv_sem=recv_sem.at[c, k],
            device_id={"tile": there},
            device_id_type=MESH,
        )

    def own_copy(c):
        return pltpu.make_async_copy(send.at[c, me], recv.at[c, me], own_sem.at[c])

    for r in range(2):
        for b in range(WIDE // LANES):
            taps = fir_ref[:, b * LANES : (b + 1) * LANES]
            both = dft_ref[r][:, None, :] * taps[None]
            filt[:, r * WIDE + b * LANES : r * WIDE + (b + 1) * LANES] = both.reshape(
                KEEP * 2 * DT, LANES
            ).astype(jnp.bfloat16)
    window[...] = jnp.zeros_like(window)
    pl.semaphore_wait(barrier, tiles - 1)
    load(0).wait()

    def channelize(c, carry):
        @pl.when(c + 1 < chunks)
        def _():
            load(c + 1).wait()

        @pl.when(c + 1 == chunks)
        def _():
            rest.wait()

        parts = []
        for f in range(2):
            for r in range(2):
                for q in range(8):
                    at = (c * 16 + f * 8 + q) * STRIDE
                    rows = slice(q * inputs, (q + 1) * inputs)
                    window[rows, r * WIDE : r * WIDE + STRIDE] = held[
                        r, :, pl.ds(pl.multiple_of(at, STRIDE), STRIDE)
                    ]
                    window[rows, r * WIDE + STRIDE : r * WIDE + STRIDE + TAIL] = held[
                        r, :, pl.ds(pl.multiple_of(at + STRIDE, STRIDE), TAIL)
                    ]
            got = lax.dot_general(
                filt[...], window[...], NT, preferred_element_type=jnp.float32
            )
            for h in range(2):
                parts.append(
                    got[:, h * LANES : (h + 1) * LANES].reshape(KEEP * 2, DT, LANES)
                )
        block = jnp.concatenate(parts, axis=1).astype(jnp.bfloat16)
        send[c] = block.reshape(tiles, chans * 2, 4 * DT, LANES)
        for k in order:
            out_copy(c, k).start()
        own_copy(c).start()
        return carry

    lax.fori_loop(0, chunks, channelize, 0)
    total[...] = jnp.zeros_like(total)

    def correlate(x, carry):
        for half in range(2):
            for k in order:
                out_copy(2 * x + half, k).wait_recv()
            own_copy(2 * x + half).wait()

        def turn(src, inner):
            rows = 4 * DT * 2
            for ch in range(chans):
                sides = []
                for p in range(2):
                    for half in range(2):
                        sides.append(recv[2 * x + half, src, ch * 2 + p])
                re0, re1, im0, im1 = sides
                one = jnp.concatenate([re0, re1, im0, im1], axis=0).T
                two = jnp.concatenate([-im0, -im1, re0, re1], axis=0).T
                place = pl.ds(pl.multiple_of(src * inputs, inputs), inputs)
                for g in range(LANES // inputs):
                    at = slice(g * 2 * rows, (g + 1) * 2 * rows)
                    left[ch, place, at] = one[g * inputs : (g + 1) * inputs]
                    right[ch, place, at] = two[g * inputs : (g + 1) * inputs]
            return inner

        lax.fori_loop(0, tiles, turn, 0)
        for ch in range(chans):
            for j in range(NBLK):
                cols = slice(j * BLOCK, (j + 1) * BLOCK)
                rhs = jnp.concatenate([left[ch, cols, :], right[ch, cols, :]], axis=0)
                got = lax.dot_general(
                    left[ch, : (j + 1) * BLOCK, :],
                    rhs,
                    NT,
                    preferred_element_type=jnp.float32,
                )
                for i in range(j + 1):
                    q = ch * NPAIR + i * NBLK - i * (i - 1) // 2 + j - i
                    for p in range(2):
                        total[q, p] += got[
                            i * BLOCK : (i + 1) * BLOCK, p * BLOCK : (p + 1) * BLOCK
                        ]
        return carry

    lax.fori_loop(0, chunks // 2, correlate, 0)

    scale = 1.0 / (chunks * 16 * DT)
    for p in range(NPAIR):
        q = layout_ref[p]
        for ch in range(chans):
            out_ref[ch * NPAIR + p] = total[ch * NPAIR + q] * scale

    def drain(c, carry):
        for k in order:
            out_copy(c, k).wait_send()
        return carry

    lax.fori_loop(0, chunks, drain, 0)


def fused(samples, fir_taps, chan_map, layout):
    tiles = lax.axis_size("tile")
    inputs = samples.shape[1]
    spec_count = samples.shape[2] // NCHAN - TAPS + 1
    chunks = spec_count // (16 * DT)
    chans = KEEP // tiles
    table = dft_table(chan_map).astype(jnp.float32)
    table = table.transpose(0, 3, 2, 1).reshape(2, KEEP * 2, NCHAN)
    table = jnp.concatenate([table, table], axis=2)
    fir = jnp.stack(
        [jnp.pad(fir_taps, ((dt, DT - dt), (0, 0))).reshape(WIDE) for dt in range(DT)]
    )
    half = 4 * DT
    blocks = (chunks, tiles, chans * 2, half, LANES)
    turned = (chans, tiles * inputs, 4 * half * LANES // inputs)
    result = (chans * NPAIR, 2, BLOCK, BLOCK)
    vmem = pl.BlockSpec(memory_space=pltpu.VMEM)
    return pl.pallas_call(
        functools.partial(kernel, tiles, chunks),
        out_shape=jax.ShapeDtypeStruct(result, jnp.float32),
        in_specs=[
            pl.BlockSpec(memory_space=pltpu.SMEM),
            vmem,
            vmem,
            pl.BlockSpec(memory_space=pl.ANY),
        ],
        out_specs=vmem,
        scratch_shapes=[
            pltpu.VMEM(samples.shape, jnp.bfloat16),
            pltpu.VMEM((KEEP * 2 * DT, 2 * WIDE), jnp.bfloat16),
            pltpu.VMEM((8 * inputs, 2 * WIDE), jnp.bfloat16),
            pltpu.VMEM(blocks, jnp.bfloat16),
            pltpu.VMEM(blocks, jnp.bfloat16),
            pltpu.VMEM(turned, jnp.bfloat16),
            pltpu.VMEM(turned, jnp.bfloat16),
            pltpu.VMEM(result, jnp.float32),
            pltpu.SemaphoreType.DMA((chunks + 1,)),
            pltpu.SemaphoreType.DMA((chunks,)),
            pltpu.SemaphoreType.DMA((chunks, tiles)),
            pltpu.SemaphoreType.DMA((chunks, tiles)),
        ],
        compiler_params=pltpu.CompilerParams(
            collective_id=0,
            has_side_effects=True,
            vmem_limit_bytes=48 * 1024 * 1024,
        ),
    )(layout, table, fir, samples)


def plain(samples, fir_taps, chan_map, layout):
    tiles = lax.axis_size("tile")
    inputs = samples.shape[1]
    spec_count = samples.shape[2] // NCHAN - TAPS + 1
    summed = jnp.zeros((2, inputs, spec_count * NCHAN), jnp.float32)
    for k in range(TAPS):
        part = lax.slice_in_dim(samples, k * NCHAN, (k + spec_count) * NCHAN, axis=2)
        summed = summed + part.astype(jnp.float32) * jnp.tile(fir_taps[k], spec_count)
    weighted = summed.astype(jnp.bfloat16).reshape(2, inputs, spec_count, NCHAN)
    spectra = jnp.einsum(
        "rnqc,ritn->ciqt", dft_table(chan_map), weighted, preferred_element_type=jnp.float32
    ).astype(jnp.bfloat16)
    rows = KEEP * NPAIR // tiles
    held = max(1, rows // NPAIR)
    spectra = jnp.repeat(spectra, max(1, NPAIR // rows), axis=0)
    spectra = spectra.reshape(tiles, held, inputs, 2, spec_count)
    got = lax.all_to_all(spectra, "tile", split_axis=0, concat_axis=2, tiled=True)
    got = got.reshape(held, tiles * inputs, 2, spec_count)
    swapped = jnp.stack([-got[:, :, 1], got[:, :, 0]], 2)
    first, second = pair_tables(NBLK)
    kinds = [
        jnp.einsum("capt,cbpt->cab", got, side, preferred_element_type=jnp.float32)
        for side in (got, swapped)
    ]
    blocks = jnp.stack(
        [
            jnp.stack(
                [
                    kind[:, i * BLOCK : (i + 1) * BLOCK, j * BLOCK : (j + 1) * BLOCK]
                    for kind in kinds
                ],
                1,
            )
            for i, j in zip(first, second)
        ],
        1,
    )
    start = lax.axis_index("tile") * rows % NPAIR
    out = []
    for row in range(rows):
        spot = (start + row) % NPAIR
        pair = jnp.sum(jnp.where(jnp.arange(NPAIR) == spot, layout, 0))
        chosen = (jnp.arange(NPAIR) == pair)[:, None, None, None]
        out.append(jnp.sum(jnp.where(chosen, blocks[row // NPAIR], 0.0), 0))
    return jnp.stack(out) / spec_count


def on_device(samples, fir_taps, chan_map, layout):
    tiles = lax.axis_size("tile")
    inputs = samples.shape[1]
    spec_count = samples.shape[2] // NCHAN - TAPS + 1
    fits = tiles == 16 and inputs == 32 and spec_count % (32 * DT) == 0
    return (fused if fits and spec_count <= 1024 else plain)(
        samples, fir_taps, chan_map, layout
    )


def solution(mesh):
    placed = (P(None, ("group", "tile"), None), P(), P(), P())
    return jax.shard_map(
        on_device,
        mesh=mesh,
        in_specs=placed,
        out_specs=P(("group", "tile"), None, None, None),
        check_vma=False,
    )
```

time: 226 us -> 110 us (0.49)
  the two profiles are of different devices: /device:TPU:15 before, /device:TPU:0 now
where the time goes in v1:
time: 110 us
  Pallas kernels  105 us (95%)
  local copies, waits for them, and re-layouts  3.84 us (3%)
    pallas_call x1, Pallas kernels, fused(): pl.pallas_call(functools.partial(kernel, tiles, chunks), out_shape=jax.Sh...  105 us

profile of v1, /device:TPU:0, one launch (start us, length us, event | category | flops | bytes accessed | tf_op | source)
XLA Modules:
  0.0 109.5 jit_solution(13945883254765280754)
XLA Ops:
  0.0 0.8 negate_convert_fusion
  0.9 0.1 maximum_convert_fusion.dft_ref
  1.0 1.0 fusion.7
  2.0 0.1 stack_reshape.31
  2.0 0.1 stack_reshape.29
  2.1 0.1 stack_reshape.28
  2.2 0.1 stack_reshape.27
  2.3 0.1 stack_reshape.26
  2.3 0.1 stack_reshape.25
  2.4 0.1 stack_reshape.24
  2.5 0.1 stack_reshape.30
  2.6 0.1 stack.32.fir_ref
  2.6 0.0 copy-start
  2.7 0.6 copy-done
  3.3 104.7 %shard_map.46 = f32[20,2,128,128]{3,2,1,0:T(8,128)S(1)} custom-call(s32[10]{0:T(128)S(1)} %copy-done, f32[2,64,128]{2,1,0:T(8,128)S(1)} %maximum_convert_fusion.dft_ref, f32[8,1024]{1,0:T(8,128)S(1)} %stack.32.fir_ref, bf16[2,32,65984]{2,1,0:T(8,128)(2,1)} %samples_ref.1), custom_call_target="tpu_custom_call" | custom-call | tf_op jit(solution)/shard_map/pallas_call | solution.py:239
  108.0 1.5 %copy.7 = f32[20,2,128,128]{3,2,1,0:T(8,128)} copy(f32[20,2,128,128]{3,2,1,0:T(8,128)S(1)} %shard_map.46) | data formatting | bytes 5242880
  (3 shorter events, 0.0 us)
Async XLA Ops:
  2.6 0.7 copy-start

commit v2 on v1

--- a/solution.py
+++ b/solution.py
@@ -53,11 +53,12 @@
     tiles,
     chunks,
     layout_ref,
-    dft_ref,
+    chan_ref,
     fir_ref,
     samples_ref,
     out_ref,
     held,
+    spread,
     filt,
     window,
     send,
@@ -74,7 +75,7 @@
     me = lax.axis_index("tile")
     per = 16 * STRIDE
     inputs = samples_ref.shape[1]
-    order = sorted(range(1, tiles), reverse=True)
+    order = list(range(1, tiles))
     chans = KEEP // tiles
 
     def load(c):
@@ -92,6 +93,7 @@
         load(c).start()
     rest.start()
 
+    spread[...] = jnp.zeros_like(spread)
     barrier = pltpu.get_barrier_semaphore()
     for k in order:
         pl.semaphore_signal(
@@ -112,10 +114,26 @@
     def own_copy(c):
         return pltpu.make_async_copy(send.at[c, me], recv.at[c, me], own_sem.at[c])
 
+    tap_index = lax.broadcasted_iota(jnp.int32, (KEEP * 2, LANES), 1) & (NCHAN - 1)
+    is_imag = lax.broadcasted_iota(jnp.int32, (KEEP * 2, LANES), 0) & 1 == 1
+    angles = (tap_index * chan_ref[...] & (NCHAN - 1)).astype(jnp.float32) * (
+        2.0 * math.pi / NCHAN
+    )
+    cosine = jnp.cos(angles) * (1.0 / math.sqrt(NCHAN))
+    sine_part = jnp.sin(angles) * (1.0 / math.sqrt(NCHAN))
+    table = [
+        jnp.where(is_imag, -sine_part, cosine),
+        jnp.where(is_imag, cosine, sine_part),
+    ]
+    table = [side.astype(jnp.bfloat16).astype(jnp.float32) for side in table]
+    for dt in range(DT):
+        for k in range(TAPS):
+            at = (dt + k) * NCHAN
+            spread[dt : dt + 1, at : at + NCHAN] = fir_ref[k : k + 1, :]
     for r in range(2):
         for b in range(WIDE // LANES):
-            taps = fir_ref[:, b * LANES : (b + 1) * LANES]
-            both = dft_ref[r][:, None, :] * taps[None]
+            taps = spread[:, b * LANES : (b + 1) * LANES]
+            both = table[r][:, None, :] * taps[None]
             filt[:, r * WIDE + b * LANES : r * WIDE + (b + 1) * LANES] = both.reshape(
                 KEEP * 2 * DT, LANES
             ).astype(jnp.bfloat16)
@@ -225,12 +243,8 @@
     spec_count = samples.shape[2] // NCHAN - TAPS + 1
     chunks = spec_count // (16 * DT)
     chans = KEEP // tiles
-    table = dft_table(chan_map).astype(jnp.float32)
-    table = table.transpose(0, 3, 2, 1).reshape(2, KEEP * 2, NCHAN)
-    table = jnp.concatenate([table, table], axis=2)
-    fir = jnp.stack(
-        [jnp.pad(fir_taps, ((dt, DT - dt), (0, 0))).reshape(WIDE) for dt in range(DT)]
-    )
+    rows = jnp.repeat(chan_map, 2).reshape(KEEP * 2, 1)
+    rows = jnp.broadcast_to(rows, (KEEP * 2, LANES))
     half = 4 * DT
     blocks = (chunks, tiles, chans * 2, half, LANES)
     turned = (chans, tiles * inputs, 4 * half * LANES // inputs)
@@ -248,6 +262,7 @@
         out_specs=vmem,
         scratch_shapes=[
             pltpu.VMEM(samples.shape, jnp.bfloat16),
+            pltpu.VMEM((DT, WIDE), jnp.float32),
             pltpu.VMEM((KEEP * 2 * DT, 2 * WIDE), jnp.bfloat16),
             pltpu.VMEM((8 * inputs, 2 * WIDE), jnp.bfloat16),
             pltpu.VMEM(blocks, jnp.bfloat16),
@@ -265,7 +280,7 @@
             has_side_effects=True,
             vmem_limit_bytes=48 * 1024 * 1024,
         ),
-    )(layout, table, fir, samples)
+    )(layout, rows, fir_taps, samples)
 
 
 def plain(samples, fir_taps, chan_map, layout):

time: 110 us -> 106 us (0.964)
  the two profiles are of different devices: /device:TPU:0 before, /device:TPU:15 now
where the time goes in v2:
time: 106 us
  Pallas kernels  102 us (96%)
  local copies, waits for them, and re-layouts  3.75 us (4%)
    pallas_call x1, Pallas kernels, fused(): pl.pallas_call(functools.partial(kernel, tiles, chunks), out_shape=jax.Sh...  102 us
    unnamed x5, local copies, waits for them, and re-layouts  2.85 us

profile of v2, /device:TPU:15, one launch (start us, length us, event | category | flops | bytes accessed | tf_op | source)
XLA Modules:
  0.0 106.1 jit_solution(3171345147923017867)
XLA Ops:
  0.0 0.7 broadcast_in_dim.10
  0.7 0.1 broadcast_in_dim.11
  0.8 0.1 broadcast_in_dim.12.chan_ref
  0.9 0.0 copy-start
  0.9 0.7 copy-done
  1.6 0.0 copy-start.1
  1.6 0.7 copy-done.1
  2.3 102.4 %shard_map.46 = f32[20,2,128,128]{3,2,1,0:T(8,128)S(1)} custom-call(s32[10]{0:T(128)S(1)} %copy-done.1, s32[64,128]{1,0:T(8,128)S(1)} %broadcast_in_dim.12.chan_ref, f32[8,64]{1,0:T(8,128)S(1)} %copy-done, bf16[2,32,65984]{2,1,0:T(8,128)(2,1)} %samples_ref.1), custom_call_target="tpu_custom_call" | custom-call | tf_op jit(solution)/shard_map/pallas_call | solution.py:253
  104.6 1.5 %copy.6 = f32[20,2,128,128]{3,2,1,0:T(8,128)} copy(f32[20,2,128,128]{3,2,1,0:T(8,128)S(1)} %shard_map.46) | data formatting | bytes 5242880
Async XLA Ops:
  0.9 0.7 copy-start
  1.6 0.7 copy-start.1

commit v3 on v2

--- a/solution.py
+++ b/solution.py
@@ -202,7 +202,7 @@
                     right[ch, place, at] = two[g * inputs : (g + 1) * inputs]
             return inner
 
-        lax.fori_loop(0, tiles, turn, 0)
+        lax.fori_loop(0, tiles, turn, 0, unroll=4)
         for ch in range(chans):
             for j in range(NBLK):
                 cols = slice(j * BLOCK, (j + 1) * BLOCK)

time: 106 us -> 106 us (level)
  no operation moved by 1% of the time
where the time goes in v3:
time: 106 us; the launch traced here: 105 us
  Pallas kernels  102 us (96%)
  local copies, waits for them, and re-layouts  3.75 us (4%)
    pallas_call x1, Pallas kernels, fused(): pl.pallas_call(functools.partial(kernel, tiles, chunks), out_shape=jax.Sh...  102 us
    unnamed x5, local copies, waits for them, and re-layouts  2.85 us

profile of v3, /device:TPU:15, one launch (start us, length us, event | category | flops | bytes accessed | tf_op | source)
XLA Modules:
  0.0 105.5 jit_solution(1879980837358216070)
XLA Ops:
  0.0 0.7 broadcast_in_dim.10
  0.7 0.1 broadcast_in_dim.11
  0.8 0.1 broadcast_in_dim.12.chan_ref
  0.9 0.0 copy-start
  0.9 0.7 copy-done
  1.6 0.0 copy-start.1
  1.6 0.7 copy-done.1
  2.3 101.7 %shard_map.46 = f32[20,2,128,128]{3,2,1,0:T(8,128)S(1)} custom-call(s32[10]{0:T(128)S(1)} %copy-done.1, s32[64,128]{1,0:T(8,128)S(1)} %broadcast_in_dim.12.chan_ref, f32[8,64]{1,0:T(8,128)S(1)} %copy-done, bf16[2,32,65984]{2,1,0:T(8,128)(2,1)} %samples_ref.1), custom_call_target="tpu_custom_call" | custom-call | tf_op jit(solution)/shard_map/pallas_call | solution.py:253
  104.0 1.5 %copy.6 = f32[20,2,128,128]{3,2,1,0:T(8,128)} copy(f32[20,2,128,128]{3,2,1,0:T(8,128)S(1)} %shard_map.46) | data formatting | bytes 5242880
Async XLA Ops:
  0.9 0.7 copy-start
  1.6 0.7 copy-start.1
